TPU v7x, 32 devices: a whole 2x2x4 slice. The times are simulated.
32 devices in a mesh: quad: 16 (over z, x, core), rows: 2 (over y).
Axes of the slice: x: 2, y: 2, z: 4, core: 2. Of those that a mesh axis runs over, the one named last changes fastest.
Arguments:
- solutions: bfloat16 [32, 2, 64, 16, 1280], P('quad', None, None, None, 'rows'), may hold values from -64 to 64
- angles: float32 [32], replicated, may hold values from -3.140625 to 3.140625
- qweights: float32 [2, 32], replicated, may hold values from -1 to 1
- neighbours: int32 [320, 8], P(('quad', 'rows')), may hold values from 0 to 319, as said below
- hblocks: bfloat16 [320, 64, 512], P(('quad', 'rows')), may hold values from -0.25 to 0.25
Outputs:
- h_moments: bfloat16 [1024, 20480], P(None, ('quad', 'rows'))
- ritz_matrices: float32 [512, 2, 2, 512], P('quad')
Inputs may be any that keep to these rules, and one draw needn't show every extreme that they name: neighbours[c, 0] = c, neighbours[c, 1] = min(c + 2, 319), neighbours[c, 2] = max(c - 2, 0); every entry lies within 2 of c.
All inputs are finite; a program needn't handle non-finite values.
Results may differ from a plain program's by a relative error of at most 0.0075.
Values may be sent and summed in bfloat16 or wider, within the bound.
A program may use at most 64 MiB of HBM per device.

v0:
```python
import jax
import jax.numpy as jnp
from jax import lax
from jax.sharding import PartitionSpec as P

LCOL = 64
QPTS = 32
KMOM = 8
NB = 8
HALO = 2


def extended(block, sides, width):
    for axis, dim in sides:
        count = lax.axis_size(axis)
        forward = [(i, i + 1) for i in range(count - 1)]
        backward = [(target, source) for source, target in forward]
        low = lax.ppermute(
            lax.slice_in_dim(block, block.shape[dim] - width, None, axis=dim), axis, forward
        )
        high = lax.ppermute(lax.slice_in_dim(block, 0, width, axis=dim), axis, backward)
        block = jnp.concatenate([low, block, high], axis=dim)
    return block


def moment_coefficients(angles, qweights):
    order = jnp.arange(KMOM, dtype=jnp.float32)[:, None]
    phase = order * angles[None, :]
    cosine = jnp.cos(phase)
    sine = jnp.sin(phase)
    real_coef = qweights[0][None, :] * cosine - qweights[1][None, :] * sine
    imag_coef = qweights[0][None, :] * sine + qweights[1][None, :] * cosine
    real_rows = jnp.stack([real_coef, -imag_coef], -1)
    imag_rows = jnp.stack([imag_coef, real_coef], -1)
    mixing = jnp.stack([real_rows, imag_rows], 0)
    return mixing.reshape(2 * KMOM, 2 * QPTS).astype(jnp.bfloat16)


def split_parts(product, half_cols, row_count):
    real_part = product[:row_count, :half_cols] + product[row_count:, half_cols:]
    imag_part = product[:row_count, half_cols:] - product[row_count:, :half_cols]
    return jnp.stack([real_part, imag_part], 1)


def gram_part(moments, applied, first_row, row_count, total_rows):
    half_cols = moments.shape[0] // 2
    chosen = jnp.concatenate(
        [
            lax.dynamic_slice_in_dim(moments, first_row, row_count, 0),
            lax.dynamic_slice_in_dim(moments, half_cols + first_row, row_count, 0),
        ],
        0,
    )
    contract = (((1,), (1,)), ((), ()))
    plain = lax.dot_general(chosen, moments, contract, preferred_element_type=jnp.float32)
    mixed = lax.dot_general(chosen, applied, contract, preferred_element_type=jnp.float32)
    ritz = jnp.stack(
        [split_parts(plain, half_cols, row_count), split_parts(mixed, half_cols, row_count)], 1
    )
    return ritz * (1.0 / total_rows)


def per_device(solutions, angles, qweights, neighbours, hblocks):
    groups = lax.axis_size("quad") * lax.axis_size("rows")
    rows_dev = solutions.shape[4]
    cells_dev = hblocks.shape[0]
    orbitals = hblocks.shape[1]
    half_cols = KMOM * LCOL
    mixing = moment_coefficients(angles, qweights)
    received = lax.all_to_all(solutions, "quad", split_axis=3, concat_axis=0, tiled=True)
    stacked = received.reshape(QPTS * 2, LCOL, received.shape[4])
    result = jnp.einsum("pq,qln->pln", mixing, stacked, preferred_element_type=jnp.float32)
    moments = result.reshape(2 * half_cols, received.shape[4]).astype(jnp.bfloat16)
    padded = extended(moments, ((("quad", "rows"), 1),), HALO * orbitals)
    first_cell = (
        lax.axis_index("quad") * lax.axis_size("rows") + lax.axis_index("rows")
    ) * cells_dev
    local_index = (neighbours - first_cell + HALO).reshape(-1)
    cellwise = padded.reshape(2 * half_cols, cells_dev + 2 * HALO, orbitals)
    nearby = jnp.take(cellwise, local_index, axis=1).reshape(
        2 * half_cols, cells_dev, NB * orbitals
    )
    applied = jnp.einsum("cam,xcm->xca", hblocks, nearby, preferred_element_type=jnp.float32)
    applied = applied.reshape(2 * half_cols, rows_dev).astype(jnp.bfloat16)
    total_rows = rows_dev * groups
    share_rows = half_cols // lax.axis_size("quad")
    summed = lax.psum(gram_part(moments, applied, 0, half_cols, total_rows), ("quad", "rows"))
    ritz_matrices = lax.dynamic_slice_in_dim(
        summed, lax.axis_index("quad") * share_rows, share_rows, 0
    )
    return (applied, ritz_matrices)


def solution(mesh):
    in_specs = (
        P("quad", None, None, None, "rows"),
        P(),
        P(),
        P(("quad", "rows"), None),
        P(("quad", "rows"), None, None),
    )
    out_specs = (P(None, ("quad", "rows")), P("quad", None, None, None))
    return jax.shard_map(
        per_device, mesh=mesh, in_specs=in_specs, out_specs=out_specs, check_vma=False
    )
```

profile of v0, /device:TPU:0, one launch (start us, length us, event | category | flops | bytes accessed | tf_op | source)
XLA Modules:
  0.0 333.4 jit_solution(11366127904357081607)
XLA Ops:
  7.2 6.2 %copy.34 = bf16[2,2,64,16,640]{4,2,1,0,3:T(8,128)(2,1)} copy(bf16[2,2,64,16,640]{4,3,2,1,0:T(8,128)(2,1)} %param.5) | data formatting | bytes 10485760 | tf_op args[0]
  13.3 7.5 %all-to-all-start = ((bf16[2,2,64,16,640]{4,2,1,0,3:T(8,128)(2,1)}), bf16[2,2,64,16,640]{4,2,1,0,3:T(8,128)(2,1)}, u32[]{:S(2)}, u32[]{:S(2)}) async-start(bf16[2,2,64,16,640]{4,2,1,0,3:T(8,128)(2,1)} %copy.34), calls=%async_computation | async-start | bytes 10485760 | tf_op jit(solution)/shard_map/all_to_all | solution.py:70
  21.8 95.1 %all-to-all-done = bf16[2,2,64,16,640]{4,2,1,0,3:T(8,128)(2,1)} async-done(((bf16[2,2,64,16,640]{4,2,1,0,3:T(8,128)(2,1)}), bf16[2,2,64,16,640]{4,2,1,0,3:T(8,128)(2,1)}, u32[]{:S(2)}, u32[]{:S(2)}) %all-to-all-start) | async-done | bytes 5242912 | tf_op jit(solution)/shard_map/all_to_all | solution.py:70
  116.8 6.5 %fusion.6 = bf16[16,64,640]{2,0,1:T(8,128)(2,1)S(1)} fusion(bf16[64,64,640]{2,1,0:T(8,128)(2,1)} %bitcast.7, bf16[16,64]{0,1:T(8,128)(2,1)S(1)} %convert_element_type.30), kind=kOutput, calls=%fused_computation.11 | convolution fusion | flops 84541440 | bytes 6555648 | tf_op jit(solution)/shard_map/pq,qln->pln/dot_general | solution.py:72
  123.3 0.3 copy.37
  123.7 1.8 fusion.23
  125.5 3.4 %collective-permute-start = (bf16[1024,128]{1,0:T(8,128)(2,1)S(1)}, bf16[1024,128]{1,0:T(8,128)(2,1)S(1)}, u32[]{:S(2)}, u32[]{:S(2)}) collective-permute-start(bf16[1024,128]{1,0:T(8,128)(2,1)S(1)} %get-tuple-element.14), channel_id=1, source_target_pairs={{0,1},{1,2},{2,3},{3,4},{4,5},{5,6},{6,7},{7,8},{8,9},{9,10},{10,1... | collective-permute-start | bytes 786440 | tf_op jit(solution)/shard_map/ppermute | solution.py:18
  128.9 1.5 collective-permute-start.1
  130.4 1.5 fusion.15
  131.9 3.7 %collective-permute-done = bf16[1024,128]{1,0:T(8,128)(2,1)S(1)} collective-permute-done((bf16[1024,128]{1,0:T(8,128)(2,1)S(1)}, bf16[1024,128]{1,0:T(8,128)(2,1)S(1)}, u32[]{:S(2)}, u32[]{:S(2)}) %collective-permute-start) | collective-permute-done | bytes 262176 | tf_op jit(solution)/shard_map/ppermute | solution.py:18
  135.6 1.6 collective-permute-done.1
  137.2 1.4 pad_maximum_fusion
  138.6 2.9 copy.38
  141.5 6.3 %gather_fusion = bf16[80,1024,64]{1,2,0:T(8,128)(2,1)} fusion(bf16[1024,14,64]{0,2,1:T(8,128)(2,1)S(1)} %bitcast.45, s32[1024]{0:T(1024)S(1)} %pad_clamp_fusion), kind=kCustom, calls=%fused_computation | custom fusion | bytes 20971840 | tf_op jit(solution)/shard_map/jit(_take)/gather | solution.py:80
  147.8 5.5 %fusion.9 = bf16[10,1024,64]{1,2,0:T(8,128)(2,1)S(1)} fusion(bf16[10,64,512]{2,1,0:T(8,128)(2,1)S(1)} %copy-done, bf16[1024,10,512]{0,2,1:T(8,128)(2,1)} %bitcast.46, pred[10,512]{1,0:T(8,128)(4,1)S(1)} %broadcast_in_dim.17), kind=kOutput, calls=%fused_computation.12 | convolution fusion | flops 676986880 | bytes 12456960 | tf_op jit(solution)/shard_map/cam,xcm->xca/dot_general | solution.py:83
  153.4 1.8 fusion.24
  155.2 0.5 fusion.13
  155.7 0.7 copy-done.3
  156.4 0.4 maximum_bitcast_fusion
  156.9 2.7 maximum_multiply_fusion
  159.6 1.4 copy.41
  161.1 163.6 %all-reduce.2.cloned.1.call-done = f32[512,2,2,512]{3,0,2,1:T(8,128)} async-done(((f32[512,2,2,512]{3,0,2,1:T(8,128)}), f32[512,2,2,512]{3,0,2,1:T(8,128)}) %all-reduce.2.cloned.1.call-update) | async-done | bytes 4194320 | tf_op jit(solution)/shard_map/psum | solution.py:87
  324.7 1.0 constant_dynamic-slice_fusion
  325.6 0.9 copy.42
  (31 shorter events, 0.9 us)
Async XLA Ops:
  7.2 140.7 %copy-start = (bf16[10,64,512]{2,1,0:T(8,128)(2,1)S(1)}, bf16[10,64,512]{2,1,0:T(8,128)(2,1)}, u32[]{:S(2)}) copy-start(bf16[10,64,512]{2,1,0:T(8,128)(2,1)} %param.9) | copy-start | bytes 1966084
  13.3 7.6 %copy-start.5 = (f32[2,32]{1,0:T(2,128)S(1)}, f32[2,32]{1,0:T(2,128)}, u32[]{:S(2)}) copy-start(f32[2,32]{1,0:T(2,128)} %param.7) | copy-start | bytes 772
  13.3 7.6 %copy-start.6 = (f32[32]{0:T(128)S(1)}, f32[32]{0:T(128)}, u32[]{:S(2)}) copy-start(f32[32]{0:T(128)} %param.6) | copy-start | bytes 388
  13.3 7.9 %copy-start.4 = (s32[10,8]{0,1:T(8,128)S(1)}, s32[10,8]{0,1:T(8,128)}, u32[]{:S(2)}) copy-start(s32[10,8]{0,1:T(8,128)} %param.8) | copy-start | bytes 964
  13.3 103.5 %all-to-all-start = ((bf16[2,2,64,16,640]{4,2,1,0,3:T(8,128)(2,1)}), bf16[2,2,64,16,640]{4,2,1,0,3:T(8,128)(2,1)}, u32[]{:S(2)}, u32[]{:S(2)}) async-start(bf16[2,2,64,16,640]{4,2,1,0,3:T(8,128)(2,1)} %copy.34), calls=%async_computation | async-start | bytes 10485760 | tf_op jit(solution)/shard_map/all_to_all | solution.py:70
  20.9 303.8 %all-reduce.2.cloned.1.call-start = ((), (), s32[]{:S(2)}) async-start(), calls=%async_computation.1 | async-start | bytes 8388608 | tf_op jit(solution)/shard_map/psum | solution.py:87
  123.6 13.6 %copy-start.1 = (bf16[16,64,640]{2,1,0:T(8,128)(2,1)}, bf16[16,64,640]{2,1,0:T(8,128)(2,1)S(1)}, u32[]{:S(2)}) copy-start(bf16[16,64,640]{2,1,0:T(8,128)(2,1)S(1)} %copy.37) | copy-start | bytes 3932164
  125.5 10.1 %collective-permute-start = (bf16[1024,128]{1,0:T(8,128)(2,1)S(1)}, bf16[1024,128]{1,0:T(8,128)(2,1)S(1)}, u32[]{:S(2)}, u32[]{:S(2)}) collective-permute-start(bf16[1024,128]{1,0:T(8,128)(2,1)S(1)} %get-tuple-element.14), channel_id=1, source_target_pairs={{0,1},{1,2},{2,3},{3,4},{4,5},{5,6},{6,7},{7,8},{8,9},{9,10},{10,1... | collective-permute-start | bytes 786440 | tf_op jit(solution)/shard_map/ppermute | solution.py:18
  128.9 8.3 %collective-permute-start.1 = (bf16[1024,128]{1,0:T(8,128)(2,1)S(1)}, bf16[1024,128]{1,0:T(8,128)(2,1)S(1)}, u32[]{:S(2)}, u32[]{:S(2)}) collective-permute-start(bf16[1024,128]{1,0:T(8,128)(2,1)S(1)} %get-tuple-element.15), channel_id=1, source_target_pairs={{1,0},{2,1},{3,2},{4,3},{5,4},{6,5},{7,6},{8,7},{9,8},{10,9},{11,1... | collective-permute-start | bytes 786440 | tf_op jit(solution)/shard_map/ppermute | solution.py:21
  147.8 5.6 %copy-start.2 = (bf16[16,64,640]{2,1,0:T(8,128)(2,1)S(1)}, bf16[16,64,640]{2,1,0:T(8,128)(2,1)}, u32[]{:S(2)}) copy-start(bf16[16,64,640]{2,1,0:T(8,128)(2,1)} %copy-done.1) | copy-start | bytes 3932164
  155.2 1.2 copy-start.3
Sparse Core Ops, SparseCore 0:
  159.7 164.8 all-reduce.1
where the time goes:
time: 334 us; the launch traced here: 333 us
  waiting for transfers between devices  264 us (79%)
  local copies, waits for them, and re-layouts  20.4 us (6%)
  matrix products  15.7 us (5%)
  between operations  14.2 us (4%)
  starting transfers between devices  12.5 us (4%)
  other arithmetic  6.65 us (2%)
    psum x1, waiting for transfers between devices, per_device(): lax.psum(gram_part(moments, applied, 0, half_cols, total_rows), ('quad',...  164 us
    all_to_all x1, waiting for transfers between devices, per_device(): lax.all_to_all(solutions, 'quad', split_axis=3, concat_axis=0, tiled=True)  95.1 us
    unnamed x17, local copies, waits for them, and re-layouts  9.26 us
    all_to_all x1, starting transfers between devices, per_device(): lax.all_to_all(solutions, 'quad', split_axis=3, concat_axis=0, tiled=True)  7.53 us
  transfers between devices with their start and end apart: 4, of which 4 were waited for; matrix products, arithmetic and copies ran while one was open for 1% of the time, Pallas kernels for 0%

commit v1 on v0

--- a/solution.py
+++ b/solution.py
@@ -8,6 +8,18 @@
 KMOM = 8
 NB = 8
 HALO = 2
+
+
+def rotated_exchange(array, axis, split, join):
+    ways, here = (lax.axis_size(axis), lax.axis_index(axis))
+    width = array.shape[split] // ways
+    turned = jnp.roll(array, -here * width, axis=split)
+    got = [lax.slice_in_dim(turned, 0, width, axis=split)]
+    for far in range(1, ways):
+        sent = lax.slice_in_dim(turned, far * width, (far + 1) * width, axis=split)
+        got.append(lax.ppermute(sent, axis, [(d, (d + far) % ways) for d in range(ways)]))
+    line = jnp.concatenate(got[::-1], axis=join)
+    return jnp.roll(line, (here + 1) * got[0].shape[join], axis=join)
 
 
 def extended(block, sides, width):
@@ -67,7 +79,7 @@
     orbitals = hblocks.shape[1]
     half_cols = KMOM * LCOL
     mixing = moment_coefficients(angles, qweights)
-    received = lax.all_to_all(solutions, "quad", split_axis=3, concat_axis=0, tiled=True)
+    received = rotated_exchange(solutions, "quad", 3, 0)
     stacked = received.reshape(QPTS * 2, LCOL, received.shape[4])
     result = jnp.einsum("pq,qln->pln", mixing, stacked, preferred_element_type=jnp.float32)
     moments = result.reshape(2 * half_cols, received.shape[4]).astype(jnp.bfloat16)

time: 334 us -> 349 us (1.045)
  starting transfers between devices: 12.5 us -> 48.5 us
  waiting for transfers between devices: 264 us -> 233 us
  local copies, waits for them, and re-layouts: 20.4 us -> 27.9 us
  other arithmetic: 6.65 us -> 11.5 us
    all_to_all x1 -> x0, waiting for transfers between devices: 95.1 us -> none  [per_device(): lax.all_to_all(solutions, 'quad', split_axis=3, concat_axis=0, tiled=True)]
    ppermute x0 -> x15, waiting for transfers between devices: none -> 83.5 us  [rotated_exchange(): lax.ppermute(sent, axis, [(d, (d + far) % ways) for d in range(ways)])]
    ppermute x0 -> x15, starting transfers between devices: none -> 43.6 us  [rotated_exchange(): lax.ppermute(sent, axis, [(d, (d + far) % ways) for d in range(ways)])]
    psum x1, waiting for transfers between devices: 164 us -> 143 us  [per_device(): lax.psum(gram_part(moments, applied, 0, half_cols, total_rows), ('quad',...]
    all_to_all x1 -> x0, starting transfers between devices: 7.53 us -> none  [per_device(): lax.all_to_all(solutions, 'quad', split_axis=3, concat_axis=0, tiled=True)]
    concatenate x0 -> x1, other arithmetic: none -> 4.71 us  [rotated_exchange(): turned = jnp.roll(array, -here * width, axis=split)]
    unnamed x17 -> x50, local copies, waits for them, and re-layouts: 9.26 us -> 13.1 us
  transfers between devices with their start and end apart: 4 -> 18, of which waited for: 4 -> 12; matrix products, arithmetic and copies ran while one was open for 1% -> 1% of each run, Pallas kernels for 0% -> 0%
where the time goes in v1:
time: 349 us; the launch traced here: 348 us
  waiting for transfers between devices  233 us (67%)
  starting transfers between devices  48.5 us (14%)
  local copies, waits for them, and re-layouts  27.9 us (8%)
  between operations  14.5 us (4%)
  matrix products  13.2 us (4%)
  other arithmetic  11.5 us (3%)
    psum x1, waiting for transfers between devices, per_device(): lax.psum(gram_part(moments, applied, 0, half_cols, total_rows), ('quad',...  143 us
    ppermute x15, waiting for transfers between devices, rotated_exchange(): lax.ppermute(sent, axis, [(d, (d + far) % ways) for d in range(ways)])  83.5 us
    ppermute x15, starting transfers between devices, rotated_exchange(): lax.ppermute(sent, axis, [(d, (d + far) % ways) for d in range(ways)])  43.6 us
    unnamed x50, local copies, waits for them, and re-layouts  13.1 us
  transfers between devices with their start and end apart: 18, of which 12 were waited for; matrix products, arithmetic and copies ran while one was open for 1% of the time, Pallas kernels for 0%

profile of v1, /device:TPU:0, one launch (start us, length us, event | category | flops | bytes accessed | tf_op | source)
XLA Modules:
  0.0 348.3 jit_solution(10654998847310142290)
XLA Ops:
  7.2 6.1 %copy.34 = bf16[2,2,64,16,640]{4,2,3,1,0:T(8,128)(2,1)} copy(bf16[2,2,64,16,640]{4,3,2,1,0:T(8,128)(2,1)} %param.5) | data formatting | bytes 10485760 | tf_op args[0]
  13.4 4.7 %fusion.3 = bf16[2,2,64,16,640]{4,2,3,1,0:T(8,128)(2,1)S(1)} fusion(s32[]{:T(128)S(6)} %select_n.50, bf16[2,2,64,16,640]{4,2,3,1,0:T(8,128)(2,1)} %copy.34), kind=kLoop, calls=%fused_computation.6 | loop fusion | flops 2621440 | bytes 10485764 | tf_op jit(solution)/shard_map/jit(_roll_dynamic)/concatenate | solution.py:16
  18.1 2.3 copy-done.1
  20.4 2.0 fusion.23
  22.4 5.4 %collective-permute-start = (bf16[2,2,64,1,640]{4,2,3,1,0:T(8,128)(2,1)}, bf16[2,2,64,1,640]{4,2,3,1,0:T(8,128)(2,1)S(1)}, u32[]{:S(2)}, u32[]{:S(2)}) collective-permute-start(bf16[2,2,64,1,640]{4,2,3,1,0:T(8,128)(2,1)} %get-tuple-element.24), channel_id=1, source_target_pairs={{0,30},{2,0},{4,2},{6,4},{8,6},{10,8},{12,10},{14,12},{16,14},{18,... | collective-permute-start | bytes 983048 | tf_op jit(solution)/shard_map/ppermute | solution.py:20
  30.0 6.2 %collective-permute-done = bf16[2,2,64,1,640]{4,2,3,1,0:T(8,128)(2,1)S(1)} collective-permute-done((bf16[2,2,64,1,640]{4,2,3,1,0:T(8,128)(2,1)}, bf16[2,2,64,1,640]{4,2,3,1,0:T(8,128)(2,1)S(1)}, u32[]{:S(2)}, u32[]{:S(2)}) %collective-permute-start) | collective-permute-done | bytes 327712 | tf_op jit(solution)/shard_map/ppermute | solution.py:20
  36.2 7.0 %collective-permute-done.1 = bf16[2,2,64,1,640]{4,2,3,1,0:T(8,128)(2,1)S(1)} collective-permute-done((bf16[2,2,64,1,640]{4,2,3,1,0:T(8,128)(2,1)}, bf16[2,2,64,1,640]{4,2,3,1,0:T(8,128)(2,1)S(1)}, u32[]{:S(2)}, u32[]{:S(2)}) %collective-permute-start.1) | collective-permute-done | bytes 327712 | tf_op jit(solution)/shard_map/ppermute | solution.py:20
  43.3 7.0 %collective-permute-done.2 = bf16[2,2,64,1,640]{4,2,3,1,0:T(8,128)(2,1)S(1)} collective-permute-done((bf16[2,2,64,1,640]{4,2,3,1,0:T(8,128)(2,1)}, bf16[2,2,64,1,640]{4,2,3,1,0:T(8,128)(2,1)S(1)}, u32[]{:S(2)}, u32[]{:S(2)}) %collective-permute-start.2) | collective-permute-done | bytes 327712 | tf_op jit(solution)/shard_map/ppermute | solution.py:20
  50.3 7.0 %collective-permute-done.3 = bf16[2,2,64,1,640]{4,2,3,1,0:T(8,128)(2,1)S(1)} collective-permute-done((bf16[2,2,64,1,640]{4,2,3,1,0:T(8,128)(2,1)}, bf16[2,2,64,1,640]{4,2,3,1,0:T(8,128)(2,1)S(1)}, u32[]{:S(2)}, u32[]{:S(2)}) %collective-permute-start.3) | collective-permute-done | bytes 327712 | tf_op jit(solution)/shard_map/ppermute | solution.py:20
  57.3 7.0 %collective-permute-done.4 = bf16[2,2,64,1,640]{4,2,3,1,0:T(8,128)(2,1)S(1)} collective-permute-done((bf16[2,2,64,1,640]{4,2,3,1,0:T(8,128)(2,1)}, bf16[2,2,64,1,640]{4,2,3,1,0:T(8,128)(2,1)S(1)}, u32[]{:S(2)}, u32[]{:S(2)}) %collective-permute-start.4) | collective-permute-done | bytes 327712 | tf_op jit(solution)/shard_map/ppermute | solution.py:20
  64.3 7.0 %collective-permute-done.5 = bf16[2,2,64,1,640]{4,2,3,1,0:T(8,128)(2,1)S(1)} collective-permute-done((bf16[2,2,64,1,640]{4,2,3,1,0:T(8,128)(2,1)}, bf16[2,2,64,1,640]{4,2,3,1,0:T(8,128)(2,1)S(1)}, u32[]{:S(2)}, u32[]{:S(2)}) %collective-permute-start.5) | collective-permute-done | bytes 327712 | tf_op jit(solution)/shard_map/ppermute | solution.py:20
  71.3 22.4 %collective-permute-start.10 = (bf16[2,2,64,1,640]{4,2,3,1,0:T(8,128)(2,1)}, bf16[2,2,64,1,640]{4,2,3,1,0:T(8,128)(2,1)S(1)}, u32[]{:S(2)}, u32[]{:S(2)}) collective-permute-start(bf16[2,2,64,1,640]{4,2,3,1,0:T(8,128)(2,1)} %get-tuple-element.14), channel_id=1, source_target_pairs={{0,10},{2,12},{4,14},{6,16},{8,18},{10,20},{12,22},{14,24},{16,26}... | collective-permute-start | bytes 983048 | tf_op jit(solution)/shard_map/ppermute | solution.py:20
  93.8 14.1 %collective-permute-start.11 = (bf16[2,2,64,1,640]{4,2,3,1,0:T(8,128)(2,1)}, bf16[2,2,64,1,640]{4,2,3,1,0:T(8,128)(2,1)S(1)}, u32[]{:S(2)}, u32[]{:S(2)}) collective-permute-start(bf16[2,2,64,1,640]{4,2,3,1,0:T(8,128)(2,1)} %get-tuple-element.13), channel_id=1, source_target_pairs={{0,8},{2,10},{4,12},{6,14},{8,16},{10,18},{12,20},{14,22},{16,24},... | collective-permute-start | bytes 983048 | tf_op jit(solution)/shard_map/ppermute | solution.py:20
  107.9 29.9 %collective-permute-done.7 = bf16[2,2,64,1,640]{4,2,3,1,0:T(8,128)(2,1)S(1)} collective-permute-done((bf16[2,2,64,1,640]{4,2,3,1,0:T(8,128)(2,1)}, bf16[2,2,64,1,640]{4,2,3,1,0:T(8,128)(2,1)S(1)}, u32[]{:S(2)}, u32[]{:S(2)}) %collective-permute-start.7) | collective-permute-done | bytes 327712 | tf_op jit(solution)/shard_map/ppermute | solution.py:20
  138.4 7.7 %collective-permute-done.12 = bf16[2,2,64,1,640]{4,2,3,1,0:T(8,128)(2,1)S(1)} collective-permute-done((bf16[2,2,64,1,640]{4,2,3,1,0:T(8,128)(2,1)S(1)}, bf16[2,2,64,1,640]{4,2,3,1,0:T(8,128)(2,1)S(1)}, u32[]{:S(2)}, u32[]{:S(2)}) %collective-permute-start.12) | collective-permute-done | bytes 327712 | tf_op jit(solution)/shard_map/ppermute | solution.py:20
  146.1 4.8 %collective-permute-done.13 = bf16[2,2,64,1,640]{4,2,3,1,0:T(8,128)(2,1)S(1)} collective-permute-done((bf16[2,2,64,1,640]{4,2,3,1,0:T(8,128)(2,1)S(1)}, bf16[2,2,64,1,640]{4,2,3,1,0:T(8,128)(2,1)S(1)}, u32[]{:S(2)}, u32[]{:S(2)}) %collective-permute-start.13) | collective-permute-done | bytes 327712 | tf_op jit(solution)/shard_map/ppermute | solution.py:20
  154.6 4.0 %fusion.7 = bf16[16,64,640]{2,0,1:T(8,128)(2,1)S(1)} fusion(bf16[64,64,640]{2,1,0:T(8,128)(2,1)S(1)} %bitcast.43, bf16[16,64]{0,1:T(8,128)(2,1)S(1)} %convert_element_type.30), kind=kOutput, calls=%fused_computation.14 | convolution fusion | flops 84541440 | bytes 6555648 | tf_op jit(solution)/shard_map/pq,qln->pln/dot_general | solution.py:84
  160.7 3.4 collective-permute-start.15
  167.2 6.3 %collective-permute-done.15 = bf16[1024,128]{1,0:T(8,128)(2,1)S(1)} collective-permute-done((bf16[1024,128]{1,0:T(8,128)(2,1)S(1)}, bf16[1024,128]{1,0:T(8,128)(2,1)S(1)}, u32[]{:S(2)}, u32[]{:S(2)}) %collective-permute-start.15) | collective-permute-done | bytes 262176 | tf_op jit(solution)/shard_map/ppermute | solution.py:30
  175.0 2.9 copy.39
  177.8 6.3 %gather_fusion = bf16[80,1024,64]{1,2,0:T(8,128)(2,1)} fusion(bf16[1024,14,64]{0,2,1:T(8,128)(2,1)S(1)} %bitcast.41, s32[1024]{0:T(1024)S(1)} %pad_clamp_fusion), kind=kCustom, calls=%fused_computation | custom fusion | bytes 20971840 | tf_op jit(solution)/shard_map/jit(_take)/gather | solution.py:92
  184.1 5.5 %fusion.10 = bf16[10,1024,64]{1,2,0:T(8,128)(2,1)S(1)} fusion(bf16[10,64,512]{2,1,0:T(8,128)(2,1)S(1)} %copy-done, bf16[1024,10,512]{0,2,1:T(8,128)(2,1)} %bitcast.42, pred[10,512]{1,0:T(8,128)(4,1)S(1)} %broadcast_in_dim.17), kind=kOutput, calls=%fused_computation.15 | convolution fusion | flops 676986880 | bytes 12456960 | tf_op jit(solution)/shard_map/cam,xcm->xca/dot_general | solution.py:95
  192.5 2.8 maximum_multiply_fusion
  196.8 142.8 %all-reduce.2.cloned.1.call-done = f32[512,2,2,512]{3,0,2,1:T(8,128)} async-done(((f32[512,2,2,512]{3,0,2,1:T(8,128)}), f32[512,2,2,512]{3,0,2,1:T(8,128)}) %all-reduce.2.cloned.1.call-update) | async-done | bytes 4194320 | tf_op jit(solution)/shard_map/psum | solution.py:99
  (96 shorter events, 19.1 us)
Async XLA Ops:
  7.2 177.0 %copy-start = (bf16[10,64,512]{2,1,0:T(8,128)(2,1)S(1)}, bf16[10,64,512]{2,1,0:T(8,128)(2,1)}, u32[]{:S(2)}) copy-start(bf16[10,64,512]{2,1,0:T(8,128)(2,1)} %param.9) | copy-start | bytes 1966084
  7.2 332.4 %all-reduce.2.cloned.1.call-start = ((), (), s32[]{:S(2)}) async-start(), calls=%async_computation | async-start | bytes 8388608 | tf_op jit(solution)/shard_map/psum | solution.py:99
  13.4 15.8 %copy-start.5 = (s32[10,8]{0,1:T(8,128)S(1)}, s32[10,8]{0,1:T(8,128)}, u32[]{:S(2)}) copy-start(s32[10,8]{0,1:T(8,128)} %param.8) | copy-start | bytes 964
  13.4 15.8 %copy-start.6 = (f32[2,32]{1,0:T(2,128)S(1)}, f32[2,32]{1,0:T(2,128)}, u32[]{:S(2)}) copy-start(f32[2,32]{1,0:T(2,128)} %param.7) | copy-start | bytes 772
  13.4 16.0 %copy-start.7 = (f32[32]{0:T(128)S(1)}, f32[32]{0:T(128)}, u32[]{:S(2)}) copy-start(f32[32]{0:T(128)} %param.6) | copy-start | bytes 388
  22.4 13.8 %collective-permute-start = (bf16[2,2,64,1,640]{4,2,3,1,0:T(8,128)(2,1)}, bf16[2,2,64,1,640]{4,2,3,1,0:T(8,128)(2,1)S(1)}, u32[]{:S(2)}, u32[]{:S(2)}) collective-permute-start(bf16[2,2,64,1,640]{4,2,3,1,0:T(8,128)(2,1)} %get-tuple-element.24), channel_id=1, source_target_pairs={{0,30},{2,0},{4,2},{6,4},{8,6},{10,8},{12,10},{14,12},{16,14},{18,... | collective-permute-start | bytes 983048 | tf_op jit(solution)/shard_map/ppermute | solution.py:20
  27.8 15.4 %collective-permute-start.1 = (bf16[2,2,64,1,640]{4,2,3,1,0:T(8,128)(2,1)}, bf16[2,2,64,1,640]{4,2,3,1,0:T(8,128)(2,1)S(1)}, u32[]{:S(2)}, u32[]{:S(2)}) collective-permute-start(bf16[2,2,64,1,640]{4,2,3,1,0:T(8,128)(2,1)} %get-tuple-element.23), channel_id=1, source_target_pairs={{0,28},{2,30},{4,0},{6,2},{8,4},{10,6},{12,8},{14,10},{16,12},{18,... | collective-permute-start | bytes 983048 | tf_op jit(solution)/shard_map/ppermute | solution.py:20
  28.4 21.8 %collective-permute-start.2 = (bf16[2,2,64,1,640]{4,2,3,1,0:T(8,128)(2,1)}, bf16[2,2,64,1,640]{4,2,3,1,0:T(8,128)(2,1)S(1)}, u32[]{:S(2)}, u32[]{:S(2)}) collective-permute-start(bf16[2,2,64,1,640]{4,2,3,1,0:T(8,128)(2,1)} %get-tuple-element.22), channel_id=1, source_target_pairs={{0,26},{2,28},{4,30},{6,0},{8,2},{10,4},{12,6},{14,8},{16,10},{18,... | collective-permute-start | bytes 983048 | tf_op jit(solution)/shard_map/ppermute | solution.py:20
  28.7 28.6 %collective-permute-start.3 = (bf16[2,2,64,1,640]{4,2,3,1,0:T(8,128)(2,1)}, bf16[2,2,64,1,640]{4,2,3,1,0:T(8,128)(2,1)S(1)}, u32[]{:S(2)}, u32[]{:S(2)}) collective-permute-start(bf16[2,2,64,1,640]{4,2,3,1,0:T(8,128)(2,1)} %get-tuple-element.21), channel_id=1, source_target_pairs={{0,24},{2,26},{4,28},{6,30},{8,0},{10,2},{12,4},{14,6},{16,8},{18,... | collective-permute-start | bytes 983048 | tf_op jit(solution)/shard_map/ppermute | solution.py:20
  29.2 35.1 %collective-permute-start.4 = (bf16[2,2,64,1,640]{4,2,3,1,0:T(8,128)(2,1)}, bf16[2,2,64,1,640]{4,2,3,1,0:T(8,128)(2,1)S(1)}, u32[]{:S(2)}, u32[]{:S(2)}) collective-permute-start(bf16[2,2,64,1,640]{4,2,3,1,0:T(8,128)(2,1)} %get-tuple-element.20), channel_id=1, source_target_pairs={{0,22},{2,24},{4,26},{6,28},{8,30},{10,0},{12,2},{14,4},{16,6},{18... | collective-permute-start | bytes 983048 | tf_op jit(solution)/shard_map/ppermute | solution.py:20
  36.2 35.1 %collective-permute-start.5 = (bf16[2,2,64,1,640]{4,2,3,1,0:T(8,128)(2,1)}, bf16[2,2,64,1,640]{4,2,3,1,0:T(8,128)(2,1)S(1)}, u32[]{:S(2)}, u32[]{:S(2)}) collective-permute-start(bf16[2,2,64,1,640]{4,2,3,1,0:T(8,128)(2,1)} %get-tuple-element.19), channel_id=1, source_target_pairs={{0,20},{2,22},{4,24},{6,26},{8,28},{10,30},{12,0},{14,2},{16,4},{1... | collective-permute-start | bytes 983048 | tf_op jit(solution)/shard_map/ppermute | solution.py:20
  43.2 50.5 %collective-permute-start.6 = (bf16[2,2,64,1,640]{4,2,3,1,0:T(8,128)(2,1)}, bf16[2,2,64,1,640]{4,2,3,1,0:T(8,128)(2,1)S(1)}, u32[]{:S(2)}, u32[]{:S(2)}) collective-permute-start(bf16[2,2,64,1,640]{4,2,3,1,0:T(8,128)(2,1)} %get-tuple-element.18), channel_id=1, source_target_pairs={{0,18},{2,20},{4,22},{6,24},{8,26},{10,28},{12,30},{14,0},{16,2},{... | collective-permute-start | bytes 983048 | tf_op jit(solution)/shard_map/ppermute | solution.py:20
  50.2 87.6 %collective-permute-start.7 = (bf16[2,2,64,1,640]{4,2,3,1,0:T(8,128)(2,1)}, bf16[2,2,64,1,640]{4,2,3,1,0:T(8,128)(2,1)S(1)}, u32[]{:S(2)}, u32[]{:S(2)}) collective-permute-start(bf16[2,2,64,1,640]{4,2,3,1,0:T(8,128)(2,1)} %get-tuple-element.17), channel_id=1, source_target_pairs={{0,16},{2,18},{4,20},{6,22},{8,24},{10,26},{12,28},{14,30},{16,0},... | collective-permute-start | bytes 983048 | tf_op jit(solution)/shard_map/ppermute | solution.py:20
  57.3 80.6 %collective-permute-start.8 = (bf16[2,2,64,1,640]{4,2,3,1,0:T(8,128)(2,1)}, bf16[2,2,64,1,640]{4,2,3,1,0:T(8,128)(2,1)S(1)}, u32[]{:S(2)}, u32[]{:S(2)}) collective-permute-start(bf16[2,2,64,1,640]{4,2,3,1,0:T(8,128)(2,1)} %get-tuple-element.16), channel_id=1, source_target_pairs={{0,14},{2,16},{4,18},{6,20},{8,22},{10,24},{12,26},{14,28},{16,30}... | collective-permute-start | bytes 983048 | tf_op jit(solution)/shard_map/ppermute | solution.py:20
  64.3 73.7 %collective-permute-start.9 = (bf16[2,2,64,1,640]{4,2,3,1,0:T(8,128)(2,1)}, bf16[2,2,64,1,640]{4,2,3,1,0:T(8,128)(2,1)S(1)}, u32[]{:S(2)}, u32[]{:S(2)}) collective-permute-start(bf16[2,2,64,1,640]{4,2,3,1,0:T(8,128)(2,1)} %get-tuple-element.15), channel_id=1, source_target_pairs={{0,12},{2,14},{4,16},{6,18},{8,20},{10,22},{12,24},{14,26},{16,28}... | collective-permute-start | bytes 983048 | tf_op jit(solution)/shard_map/ppermute | solution.py:20
  71.3 67.0 %collective-permute-start.10 = (bf16[2,2,64,1,640]{4,2,3,1,0:T(8,128)(2,1)}, bf16[2,2,64,1,640]{4,2,3,1,0:T(8,128)(2,1)S(1)}, u32[]{:S(2)}, u32[]{:S(2)}) collective-permute-start(bf16[2,2,64,1,640]{4,2,3,1,0:T(8,128)(2,1)} %get-tuple-element.14), channel_id=1, source_target_pairs={{0,10},{2,12},{4,14},{6,16},{8,18},{10,20},{12,22},{14,24},{16,26}... | collective-permute-start | bytes 983048 | tf_op jit(solution)/shard_map/ppermute | solution.py:20
  93.8 44.6 %collective-permute-start.11 = (bf16[2,2,64,1,640]{4,2,3,1,0:T(8,128)(2,1)}, bf16[2,2,64,1,640]{4,2,3,1,0:T(8,128)(2,1)S(1)}, u32[]{:S(2)}, u32[]{:S(2)}) collective-permute-start(bf16[2,2,64,1,640]{4,2,3,1,0:T(8,128)(2,1)} %get-tuple-element.13), channel_id=1, source_target_pairs={{0,8},{2,10},{4,12},{6,14},{8,16},{10,18},{12,20},{14,22},{16,24},... | collective-permute-start | bytes 983048 | tf_op jit(solution)/shard_map/ppermute | solution.py:20
  137.8 8.3 %collective-permute-start.12 = (bf16[2,2,64,1,640]{4,2,3,1,0:T(8,128)(2,1)S(1)}, bf16[2,2,64,1,640]{4,2,3,1,0:T(8,128)(2,1)S(1)}, u32[]{:S(2)}, u32[]{:S(2)}) collective-permute-start(bf16[2,2,64,1,640]{4,2,3,1,0:T(8,128)(2,1)S(1)} %get-tuple-element.12), channel_id=1, source_target_pairs={{0,6},{2,8},{4,10},{6,12},{8,14},{10,16},{12,18},{14,20},{16,22},{... | collective-permute-start | bytes 983048 | tf_op jit(solution)/shard_map/ppermute | solution.py:20
  137.9 13.0 %collective-permute-start.13 = (bf16[2,2,64,1,640]{4,2,3,1,0:T(8,128)(2,1)S(1)}, bf16[2,2,64,1,640]{4,2,3,1,0:T(8,128)(2,1)S(1)}, u32[]{:S(2)}, u32[]{:S(2)}) collective-permute-start(bf16[2,2,64,1,640]{4,2,3,1,0:T(8,128)(2,1)S(1)} %get-tuple-element.11), channel_id=1, source_target_pairs={{0,4},{2,6},{4,8},{6,10},{8,12},{10,14},{12,16},{14,18},{16,20},{1... | collective-permute-start | bytes 983048 | tf_op jit(solution)/shard_map/ppermute | solution.py:20
  138.0 13.0 %collective-permute-start.14 = (bf16[2,2,64,1,640]{4,2,3,1,0:T(8,128)(2,1)S(1)}, bf16[2,2,64,1,640]{4,2,3,1,0:T(8,128)(2,1)S(1)}, u32[]{:S(2)}, u32[]{:S(2)}) collective-permute-start(bf16[2,2,64,1,640]{4,2,3,1,0:T(8,128)(2,1)S(1)} %get-tuple-element.10), channel_id=1, source_target_pairs={{0,2},{2,4},{4,6},{6,8},{8,10},{10,12},{12,14},{14,16},{16,18},{18... | collective-permute-start | bytes 983048 | tf_op jit(solution)/shard_map/ppermute | solution.py:20
  158.9 14.6 %copy-start.2 = (bf16[16,64,640]{2,1,0:T(8,128)(2,1)}, bf16[16,64,640]{2,1,0:T(8,128)(2,1)S(1)}, u32[]{:S(2)}) copy-start(bf16[16,64,640]{2,1,0:T(8,128)(2,1)S(1)} %copy.38) | copy-start | bytes 3932164
  160.7 12.8 %collective-permute-start.15 = (bf16[1024,128]{1,0:T(8,128)(2,1)S(1)}, bf16[1024,128]{1,0:T(8,128)(2,1)S(1)}, u32[]{:S(2)}, u32[]{:S(2)}) collective-permute-start(bf16[1024,128]{1,0:T(8,128)(2,1)S(1)} %get-tuple-element.29), channel_id=1, source_target_pairs={{0,1},{1,2},{2,3},{3,4},{4,5},{5,6},{6,7},{7,8},{8,9},{9,10},{10,1... | collective-permute-start | bytes 786440 | tf_op jit(solution)/shard_map/ppermute | solution.py:30
  164.2 9.3 %collective-permute-start.16 = (bf16[1024,128]{1,0:T(8,128)(2,1)S(1)}, bf16[1024,128]{1,0:T(8,128)(2,1)S(1)}, u32[]{:S(2)}, u32[]{:S(2)}) collective-permute-start(bf16[1024,128]{1,0:T(8,128)(2,1)S(1)} %get-tuple-element.30), channel_id=1, source_target_pairs={{1,0},{2,1},{3,2},{4,3},{5,4},{6,5},{7,6},{8,7},{9,8},{10,9},{11,1... | collective-permute-start | bytes 786440 | tf_op jit(solution)/shard_map/ppermute | solution.py:33
  184.1 5.6 %copy-start.3 = (bf16[16,64,640]{2,1,0:T(8,128)(2,1)S(1)}, bf16[16,64,640]{2,1,0:T(8,128)(2,1)}, u32[]{:S(2)}) copy-start(bf16[16,64,640]{2,1,0:T(8,128)(2,1)} %copy-done.2) | copy-start | bytes 3932164
  (2 other events, 4.6 us)
Sparse Core Ops, SparseCore 0:
  195.4 144.1 all-reduce.1
